TPU v7x, 256 devices: a whole 4x4x8 slice. The times are simulated.
256 devices in a mesh: node: 32 (over y_hi, z, core), local: 8 (over x, y_lo).
Axes of the slice: x: 4, y: 4 (y_hi: 2, y_lo: 2; y = y_hi * 2 + y_lo), z: 8, core: 2. Of those that a mesh axis runs over, the one named last changes fastest.
Arguments:
- activations: bfloat16 [2, 81920, 8192], P(None, ('node', 'local')), may hold values from -24 to 24
- cotangent: bfloat16 [2, 81920, 512], P(None, ('node', 'local')), may hold values from -6 to 6
- master: float32 [8192, 512], P('node', 'local'), may hold values from -0.0625 to 0.0625
- first_moment: float32 [8192, 512], P('node', 'local'), may hold values from -3 to 3
- second_moment: float32 [8192, 512], P('node', 'local'), may hold values from 0.05 to 2
Outputs:
- keys: bfloat16 [2, 81920, 512], P(None, ('node', 'local'))
- new_master: float32 [8192, 512], P('node', 'local')
- new_first: float32 [8192, 512], P('node', 'local')
- new_second: float32 [8192, 512], P('node', 'local')
All inputs are finite; a program needn't handle non-finite values.
Results may differ from a plain program's by a relative error of at most 0.006.
Values may be sent and summed in bfloat16 or wider, within the bound.
A program may use at most 128 MiB of HBM per device.

v0:
```python
import math

import jax
import jax.numpy as jnp
from jax import lax
from jax.sharding import PartitionSpec as P


def project_rows(rows, piece):
    return jnp.dot(rows, piece, preferred_element_type=jnp.float32).astype(jnp.bfloat16)


def per_device(activations, cotangent, master, first_moment, second_moment):
    steps = activations.shape[0]
    rows = activations.shape[1]
    weight = master.astype(jnp.bfloat16)
    secondary = lax.all_gather(weight, "node", axis=0, tiled=True)
    outputs = []
    for micro in range(steps):
        outputs.append(
            project_rows(activations[micro], lax.all_gather(secondary, "local", axis=1, tiled=True))
        )
    keys = jnp.stack(outputs)
    total = lax.dot_general(
        activations, cotangent, (((0, 1), (0, 1)), ((), ())), preferred_element_type=jnp.float32
    )
    gscale = 1.0 / math.sqrt(steps * rows * lax.axis_size("node") * lax.axis_size("local"))
    term = lax.optimization_barrier((total * gscale).astype(jnp.bfloat16)).astype(jnp.float32)
    partial_sum = lax.psum_scatter(
        term.astype(jnp.bfloat16), "local", scatter_dimension=1, tiled=True
    )
    grad = lax.psum_scatter(partial_sum, "node", scatter_dimension=0, tiled=True).astype(
        jnp.float32
    )
    new_first = 0.9 * first_moment + 0.1 * grad
    new_second = 0.95 * second_moment + 0.05 * grad * grad
    mhat = new_first / (1.0 - 0.9**10)
    vhat = new_second / (1.0 - 0.95**10)
    new_master = master - 0.0003 * (mhat / (jnp.sqrt(vhat) + 1e-08) + 0.1 * master)
    return (keys, new_master, new_first, new_second)


def solution(mesh):
    placed = (
        P(None, ("node", "local"), None),
        P(None, ("node", "local"), None),
        P("node", "local"),
        P("node", "local"),
        P("node", "local"),
    )
    return jax.shard_map(
        per_device,
        mesh=mesh,
        in_specs=placed,
        out_specs=(
            P(None, ("node", "local"), None),
            P("node", "local"),
            P("node", "local"),
            P("node", "local"),
        ),
        check_vma=False,
    )
```

profile of v0, /device:TPU:1, one launch (start us, length us, event | category | flops | bytes accessed | tf_op | source)
XLA Modules:
  0.0 593.9 jit_solution(1917026932508772252)
XLA Ops:
  7.2 0.0 copy-start
  7.2 0.0 reduce-scatter.7.cloned.1.call-start
  7.2 1.0 copy-done
  8.3 13.1 %fusion = bf16[8192,512]{1,0:T(8,128)(2,1)} fusion(bf16[2,320,8192]{2,1,0:T(8,128)(2,1)} %param.5, bf16[2,320,512]{2,1,0:T(8,128)(2,1)S(1)} %copy-done), kind=kOutput, calls=%fused_computation.1 | convolution fusion | flops 5377097728 | bytes 19529728 | tf_op jit(solution)/shard_map/dot_general | solution.py:24
  21.3 11.9 %copy.24 = bf16[8192,512]{0,1:T(8,128)(2,1)} copy(bf16[8192,512]{1,0:T(8,128)(2,1)} %fusion) | data formatting | bytes 16777216
  33.2 0.0 copy-start.1
  33.2 0.0 copy-start.2
  33.2 0.0 copy-start.3
  33.2 0.0 reduce-scatter.7.cloned.1.call-update
  33.3 0.0 reduce-scatter.5.cloned.1.call-start
  33.3 175.7 %reduce-scatter.7.cloned.1.call-done = bf16[64,8192]{1,0:T(8,128)(2,1)} async-done(((bf16[512,8192]{1,0:T(8,128)(2,1)}), bf16[64,8192]{1,0:T(8,128)(2,1)}) %reduce-scatter.7.cloned.1.call-update) | async-done | bytes 1048592
  209.0 0.0 reduce-scatter.5.cloned.1.call-update
  209.0 0.0 all-gather.3.cloned.1.call-start
  209.1 114.9 %reduce-scatter.5.cloned.1.call-done = bf16[256,64]{0,1:T(8,128)(2,1)} async-done(((bf16[8192,64]{0,1:T(8,128)(2,1)}), bf16[256,64]{0,1:T(8,128)(2,1)}) %reduce-scatter.5.cloned.1.call-update) | async-done | bytes 32784 | tf_op jit(solution)/shard_map/reduce_scatter | solution.py:32
  323.9 0.0 copy-done.1
  323.9 0.0 copy-done.2
  323.9 0.0 copy-done.3
  323.9 1.5 multiply_subtract_fusion
  325.4 0.0 all-gather.3.cloned.1.call-update
  325.4 0.0 all-gather.5.cloned.1.call-start
  325.5 77.9 %all-gather.3.cloned.1.call-done = bf16[8192,64]{0,1:T(8,128)(2,1)} async-done(((bf16[256,64]{0,1:T(8,128)(2,1)}), bf16[8192,64]{0,1:T(8,128)(2,1)}) %all-gather.3.cloned.1.call-update) | async-done | bytes 1048592 | tf_op jit(solution)/shard_map/all_gather | solution.py:17
  403.4 0.0 all-gather.5.cloned.1.call-update
  403.4 170.1 %all-gather.5.cloned.1.call-done = bf16[8192,512]{0,1:T(8,128)(2,1)} async-done(((bf16[8192,64]{0,1:T(8,128)(2,1)}), bf16[8192,512]{0,1:T(8,128)(2,1)}) %all-gather.5.cloned.1.call-update) | async-done | bytes 8388624 | tf_op jit(solution)/shard_map/all_gather | solution.py:21
  573.5 0.0 copy-start.4
  573.5 8.0 %fusion.13 = bf16[1,320,512]{2,1,0:T(8,128)(2,1)S(1)} fusion(bf16[8192,512]{0,1:T(8,128)(2,1)} %all-gather.5.cloned.1.call-done, bf16[2,320,8192]{2,1,0:T(8,128)(2,1)} %param.5), kind=kOutput, calls=%fused_computation.10 | convolution fusion | flops 2684518400 | bytes 13959168 | tf_op jit(solution)/shard_map/dot_general | solution.py:10
  581.5 0.0 copy-done.4
  581.5 5.0 fusion.16
  586.5 0.9 pad_maximum_fusion
Async XLA Ops:
  7.2 1.1 copy-start
  7.2 201.8 %reduce-scatter.7.cloned.1.call-start = ((), (), s32[]{:S(2)}) async-start(), calls=%async_computation.5 | async-start | bytes 9437184
  33.2 290.7 %copy-start.1 = (f32[256,64]{0,1:T(8,128)S(1)}, f32[256,64]{0,1:T(8,128)}, u32[]{:S(2)}) copy-start(f32[256,64]{0,1:T(8,128)} %param.7) | copy-start | bytes 196612
  33.2 290.7 %copy-start.2 = (f32[256,64]{0,1:T(8,128)S(1)}, f32[256,64]{0,1:T(8,128)}, u32[]{:S(2)}) copy-start(f32[256,64]{0,1:T(8,128)} %param.8) | copy-start | bytes 196612
  33.2 290.7 %copy-start.3 = (f32[256,64]{0,1:T(8,128)S(1)}, f32[256,64]{0,1:T(8,128)}, u32[]{:S(2)}) copy-start(f32[256,64]{0,1:T(8,128)} %param.9) | copy-start | bytes 196612
  33.3 290.7 %reduce-scatter.5.cloned.1.call-start = ((), (), s32[]{:S(2)}) async-start(), calls=%async_computation.4 | async-start | bytes 1081344 | tf_op jit(solution)/shard_map/reduce_scatter | solution.py:32
  209.0 194.4 %all-gather.3.cloned.1.call-start = ((), (), s32[]{:S(2)}) async-start(), calls=%async_computation.2 | async-start | bytes 1081344 | tf_op jit(solution)/shard_map/all_gather | solution.py:17
  325.4 248.1 %all-gather.5.cloned.1.call-start = ((), (), s32[]{:S(2)}) async-start(), calls=%async_computation.3 | async-start | bytes 9437184 | tf_op jit(solution)/shard_map/all_gather | solution.py:21
  573.5 8.0 %copy-start.4 = (bf16[8192,512]{0,1:T(8,128)(2,1)S(1)}, bf16[8192,512]{0,1:T(8,128)(2,1)}, u32[]{:S(2)}) copy-start(bf16[8192,512]{0,1:T(8,128)(2,1)} %all-gather.5.cloned.1.call-done) | copy-start | bytes 25165828
Sparse Core Ops, SparseCore 0:
  33.4 175.5 reduce-scatter.6
  213.1 110.8 reduce-scatter.4
  327.4 75.9 all-gather.2
  405.2 168.3 all-gather.4
where the time goes:
time: 598 us; the launch traced here: 594 us
  waiting for transfers between devices  539 us (90%)
  matrix products  26 us (4%)
  between operations  13.8 us (2%)
  local copies, waits for them, and re-layouts  13 us (2%)
    unnamed x5, waiting for transfers between devices  176 us
    all_gather x1, waiting for transfers between devices, per_device(): lax.all_gather(secondary, 'local', axis=1, tiled=True)  170 us
    reduce_scatter x1, waiting for transfers between devices, per_device(): lax.psum_scatter(partial_sum, 'node', scatter_dimension=0, tiled=True)  115 us
    all_gather x1, waiting for transfers between devices, per_device(): secondary = lax.all_gather(weight, 'node', axis=0, tiled=True)  77.9 us
    dot_general x1, matrix products, per_device(): lax.dot_general(activations, cotangent, (((0, 1), (0, 1)), ((), ())), pre...  13.1 us
    unnamed x11, local copies, waits for them, and re-layouts  13 us
    dot_general x2, matrix products, project_rows(): jnp.dot(rows, piece, preferred_element_type=jnp.float32)  12.9 us
  transfers between devices with their start and end apart: 4, of which 4 were waited for; matrix products, arithmetic and copies ran while one was open for 0% of the time, Pallas kernels for 0%

commit v1 on v0

v1 whole, which is shorter than its diff:
```python
import functools
import math

import jax
import jax.numpy as jnp
from jax import lax
from jax.experimental import pallas as pl
from jax.experimental.pallas import tpu as pltpu
from jax.sharding import PartitionSpec as P

BF = jnp.bfloat16
F32 = jnp.float32
MESH = pl.DeviceIdType.MESH

RS_B2, RS_C, RS_D = 0, 2, 4
AG_A, AG_B, AG_C, AG_K = 1, 3, 5, 6
P2_AT = 6


def device_of(x, y, z, c):
    return ((y // 2) * 16 + z * 2 + c, x * 2 + y % 2)


def kernel(gscale, a_hbm, c_hbm, w_ref, keys_ref, grad_ref,
           a, cb, ct, wt, g, rsib, r1ax, r1bx, r1ay, r1by, r2x, r2y, r3, acc,
           sem_a, sem_c,
           ag1s, ag1r, ag2s, ag2r, agas, agar, agbs, agbr, agcs, agcr,
           sibs, sibr, rsas, rsar, rsbs, rsbr, rs2s, rs2r, rs3s, rs3r):
    node, local = lax.axis_index("node"), lax.axis_index("local")
    c, z, yh = node % 2, (node // 2) % 8, node // 16
    x, yl = local // 2, local % 2
    y = yh * 2 + yl
    lo, hi = pl.ds(0, 128), pl.ds(128, 128)

    def at_x(d):
        return device_of((x + d) % 4, y, z, c)

    def at_y(d):
        return device_of(x, (y + d) % 4, z, c)

    def at_z(d):
        return device_of(x, y, (z + d) % 8, c)

    sibling = device_of(x, y, z, 1 - c)

    def send(src, dst, ss, rs, device):
        return pltpu.make_async_remote_copy(
            src_ref=src, dst_ref=dst, send_sem=ss, recv_sem=rs, device_id=device, device_id_type=MESH
        )

    def far_first(i):
        return (z + jnp.where(i % 2 == 1, 4 - (i + 1) // 2, 4 + i // 2)) % 8

    def near_first(i):
        return far_first(7 - i)

    barrier = pltpu.get_barrier_semaphore()
    partners = [at_x(d) for d in (1, 2, 3)] + [at_y(d) for d in (1, 2, 3)]
    partners += [at_z(d) for d in range(1, 8)] + [sibling]
    for device in partners:
        pl.semaphore_signal(barrier, inc=1, device_id=device, device_id_type=MESH)

    def load_c(m):
        return pltpu.make_async_copy(c_hbm.at[m], cb.at[pl.ds(320 * m, 320)], sem_c.at[m])

    def load_a(zz, h, m):
        block = h * 8 + zz
        return pltpu.make_async_copy(
            a_hbm.at[m, :, pl.ds(pl.multiple_of(block * 512, 512), 512)],
            a.at[block, pl.ds(320 * m, 320)],
            sem_a.at[block, m],
        )

    for m in range(2):
        load_c(m).start()

    @pl.loop(0, 8)
    def _(i):
        zz = far_first(i)
        for h in range(2):
            for m in range(2):
                load_a(zz, h, m).start()

    wt[yh, z, c, x, yl] = w_ref[...]
    pl.semaphore_wait(barrier, len(partners))

    def ag1(d):
        piece = wt.at[yh, z, c, x, yl]
        return send(piece, piece, ag1s.at[d], ag1r.at[d], at_z(d))

    for d in range(1, 8):
        ag1(d).start()

    def ag2(d):
        left = wt.at[yh, :, c, x, yl, :, lo]
        right = wt.at[yh, :, c, x, yl, :, hi]
        return (
            send(left, left, ag2s.at[0, d], ag2r.at[0, d], at_y(d)),
            send(right, right, ag2s.at[1, d], ag2r.at[1, d], at_x(d)),
        )

    def ag2_start():
        for d in range(1, 8):
            ag1(d).wait_recv()
        for d in (1, 3, 2):
            for copy in ag2(d):
                copy.start()

    def aga(zz):
        left = wt.at[:, zz, c, x, :, :, lo]
        right = wt.at[yh, zz, c, :, yl, :, hi]
        return (
            send(left, left, agas.at[0, zz], agar.at[0, zz], at_x(1)),
            send(left, left, agas.at[1, zz], agar.at[1, zz], at_x(3)),
            send(right, right, agas.at[2, zz], agar.at[2, zz], at_y(1)),
            send(right, right, agas.at[3, zz], agar.at[3, zz], at_y(3)),
        )

    def agb(zz):
        before, after = (x + 3) % 4, (x + 1) % 4
        below, above = (y + 3) % 4, (y + 1) % 4
        parts = (
            wt.at[0, zz, c, before, :, :, lo],
            wt.at[1, zz, c, after, :, :, lo],
            wt.at[below // 2, zz, c, pl.ds(0, 2), below % 2, :, hi],
            wt.at[above // 2, zz, c, pl.ds(2, 2), above % 2, :, hi],
        )
        to = (at_x(1), at_x(3), at_y(1), at_y(3))
        return tuple(
            send(parts[k], parts[k], agbs.at[k, zz], agbr.at[k, zz], to[k]) for k in range(4)
        )

    def agc(zz):
        part = wt.at[:, zz, c]
        return send(part, part, agcs.at[zz], agcr.at[zz], sibling)

    def sib(zz, h):
        return send(
            g.at[h, zz, 1 - c], rsib.at[h, zz], sibs.at[h, zz], sibr.at[h, zz], sibling
        )

    def rs_terms(i):
        zz = far_first(i)
        for h in range(2):
            for m in range(2):
                load_a(zz, h, m).wait()
            for half in range(2):
                total = jnp.dot(
                    ct[256 * half : 256 * half + 256, :], a[h * 8 + zz], preferred_element_type=F32
                )
                term = (total * gscale).astype(BF)
                for q in range(2):
                    g[h, zz, q, 2 * half : 2 * half + 2] = term[:, 256 * q : 256 * q + 256].reshape(
                        2, 2, 64, 256
                    )
            sib(zz, h).start()

    def add(*terms):
        total = terms[0].astype(F32)
        for term in terms[1:]:
            total = total + term.astype(F32)
        return total.astype(BF)

    def rsa(zz):
        far_x = (x + 2) % 4
        return (
            send(g.at[0, zz, c, far_x, :, :, lo], r1ax.at[0, zz], rsas.at[0, zz], rsar.at[0, zz], at_x(1)),
            send(g.at[1, zz, c, far_x, :, :, lo], r1ax.at[1, zz], rsas.at[1, zz], rsar.at[1, zz], at_x(3)),
            send(g.at[1 - yh, zz, c, pl.ds(0, 2), yl, :, hi], r1ay.at[0, zz], rsas.at[2, zz],
                 rsar.at[2, zz], at_y(1)),
            send(g.at[1 - yh, zz, c, pl.ds(2, 2), yl, :, hi], r1ay.at[1, zz], rsas.at[3, zz],
                 rsar.at[3, zz], at_y(3)),
        )

    def rs_pair(i):
        zz = far_first(i)
        for h in range(2):
            sib(zz, h).wait_recv()

            @pl.loop(0, 4)
            def _(k):
                g[h, zz, c, k] = add(g[h, zz, c, k], rsib[h, zz, k])

        for copy in rsa(zz):
            copy.start()

    def rsb(zz):
        before, after = (x + 3) % 4, (x + 1) % 4
        below, above = (y + 3) % 4, (y + 1) % 4
        return (
            send(g.at[:, zz, c, after, :, :, lo], r1bx.at[0, zz], rsbs.at[0, zz], rsbr.at[0, zz], at_x(1)),
            send(g.at[:, zz, c, before, :, :, lo], r1bx.at[1, zz], rsbs.at[1, zz], rsbr.at[1, zz], at_x(3)),
            send(g.at[above // 2, zz, c, :, above % 2, :, hi], r1by.at[0, zz], rsbs.at[2, zz],
                 rsbr.at[2, zz], at_y(1)),
            send(g.at[below // 2, zz, c, :, below % 2, :, hi], r1by.at[1, zz], rsbs.at[3, zz],
                 rsbr.at[3, zz], at_y(3)),
        )

    def rs_pass(i):
        zz = far_first(i)
        before, after = (x + 3) % 4, (x + 1) % 4
        below, above = (y + 3) % 4, (y + 1) % 4
        for copy in rsa(zz):
            copy.wait_recv()
        g[0, zz, c, after, :, :, lo] = add(g[0, zz, c, after, :, :, lo], r1ax[0, zz])
        g[1, zz, c, before, :, :, lo] = add(g[1, zz, c, before, :, :, lo], r1ax[1, zz])
        for k in range(2):
            g[above // 2, zz, c, k, above % 2, :, hi] = add(
                g[above // 2, zz, c, k, above % 2, :, hi], r1ay[0, zz, k]
            )
            g[below // 2, zz, c, 2 + k, below % 2, :, hi] = add(
                g[below // 2, zz, c, 2 + k, below % 2, :, hi], r1ay[1, zz, k]
            )
        for copy in rsb(zz):
            copy.start()

    def rs2(zz, d):
        to_y, to_x = (y + d) % 4, (x + d) % 4
        return (
            send(g.at[to_y // 2, zz, c, x, to_y % 2, :, lo], r2x.at[d - 1, zz], rs2s.at[0, d, zz],
                 rs2r.at[0, d, zz], at_y(d)),
            send(g.at[yh, zz, c, to_x, yl, :, hi], r2y.at[d - 1, zz], rs2s.at[1, d, zz],
                 rs2r.at[1, d, zz], at_x(d)),
        )

    def rs_second(i):
        zz = far_first(i)
        for copy in rsb(zz):
            copy.wait_recv()
        for h in range(2):
            for k in range(2):
                g[h, zz, c, x, k, :, lo] = add(
                    g[h, zz, c, x, k, :, lo], r1bx[0, zz, h, k], r1bx[1, zz, h, k]
                )
        for k in range(4):
            g[yh, zz, c, k, yl, :, hi] = add(g[yh, zz, c, k, yl, :, hi], r1by[0, zz, k], r1by[1, zz, k])
        for d in (1, 3, 2):
            for copy in rs2(zz, d):
                copy.start()

    def rs3(zz, d):
        return send(g.at[yh, zz, c, x, yl], r3.at[d], rs3s.at[d], rs3r.at[d], device_of(x, y, zz, c))

    def rs_third(i):
        zz = far_first(i)
        for d in (1, 2, 3):
            for copy in rs2(zz, d):
                copy.wait_recv()
        g[yh, zz, c, x, yl, :, lo] = add(
            g[yh, zz, c, x, yl, :, lo], r2x[0, zz], r2x[1, zz], r2x[2, zz]
        )
        g[yh, zz, c, x, yl, :, hi] = add(
            g[yh, zz, c, x, yl, :, hi], r2y[0, zz], r2y[1, zz], r2y[2, zz]
        )

        @pl.when(i < 7)
        def _():
            rs3(zz, (zz - z + 8) % 8).start()

    def project(i):
        zz = near_first(i)
        agc(zz).wait_recv()
        for h in range(2):
            piece = jnp.concatenate(
                [wt[h, zz, q].reshape(512, 256) for q in range(2)], axis=1
            )
            acc[...] += lax.dot_general(
                a[h * 8 + zz], piece, (((1,), (1,)), ((), ())), preferred_element_type=F32
            )

    def ag_a(i):
        for copy in aga(near_first(i)):
            copy.start()

    def ag_b(i):
        zz = near_first(i)
        for copy in aga(zz):
            copy.wait_recv()
        for copy in agb(zz):
            copy.start()

    def ag_c(i):
        zz = near_first(i)
        for copy in agb(zz):
            copy.wait_recv()
        agc(zz).start()

    for m in range(2):
        load_c(m).wait()
    ct[...] = cb[...].T

    @pl.loop(0, 9)
    def _(i):
        pl.when(i < 8)(lambda: rs_terms(i))
        pl.when(i >= 1)(lambda: rs_pair(i - 1))
        pl.when(i == P2_AT)(ag2_start)

    acc[...] = jnp.zeros_like(acc)

    stages = (
        (RS_B2, rs_pass), (RS_C, rs_second), (RS_D, rs_third),
        (AG_A, ag_a), (AG_B, ag_b), (AG_C, ag_c), (AG_K, project),
    )

    def ag2_wait():
        for d in range(1, 4):
            for copy in ag2(d):
                copy.wait_recv()

    @pl.loop(0, 8 + max(at for at, _ in stages))
    def _(t):
        pl.when(t == AG_A)(ag2_wait)
        for at, stage in stages:
            @pl.when((t >= at) & (t < at + 8))
            def _(stage=stage, at=at):
                stage(t - at)

    keys_ref[...] = acc[...].astype(BF).reshape(2, 320, 512)

    total = g[yh, z, c, x, yl].astype(F32)
    for d in range(1, 8):
        rs3(z, d).wait_recv()
        total = total + r3[d].astype(F32)
    grad_ref[...] = total

    for d in range(1, 8):
        ag1(d).wait_send()
        rs3(z, d).wait_send()
    for d in range(1, 4):
        for copy in ag2(d):
            copy.wait_send()

    @pl.loop(0, 8)
    def _(zz):
        for copy in (*aga(zz), *agb(zz), agc(zz), sib(zz, 0), sib(zz, 1), *rsa(zz), *rsb(zz),
                     *rs2(zz, 1), *rs2(zz, 2), *rs2(zz, 3)):
            copy.wait_send()


def per_device(activations, cotangent, master, first_moment, second_moment):
    steps, rows, width = activations.shape
    gscale = 1.0 / math.sqrt(steps * rows * lax.axis_size("node") * lax.axis_size("local"))
    piece = master.astype(BF).T
    any_spec = pl.BlockSpec(memory_space=pl.ANY)
    vmem = pl.BlockSpec(memory_space=pltpu.VMEM)
    dma = pltpu.SemaphoreType.DMA
    keys, grad = pl.pallas_call(
        functools.partial(kernel, gscale),
        out_shape=(
            jax.ShapeDtypeStruct((2, 320, 512), BF),
            jax.ShapeDtypeStruct((64, 256), F32),
        ),
        in_specs=[any_spec, any_spec, vmem],
        out_specs=(vmem, vmem),
        scratch_shapes=[
            pltpu.VMEM((16, 640, 512), BF),
            pltpu.VMEM((640, 512), BF),
            pltpu.VMEM((512, 640), BF),
            pltpu.VMEM((2, 8, 2, 4, 2, 64, 256), BF),
            pltpu.VMEM((2, 8, 2, 4, 2, 64, 256), BF),
            pltpu.VMEM((2, 8, 4, 2, 64, 256), BF),
            pltpu.VMEM((2, 8, 2, 64, 128), BF),
            pltpu.VMEM((2, 8, 2, 2, 64, 128), BF),
            pltpu.VMEM((2, 8, 2, 64, 128), BF),
            pltpu.VMEM((2, 8, 4, 64, 128), BF),
            pltpu.VMEM((3, 8, 64, 128), BF),
            pltpu.VMEM((3, 8, 64, 128), BF),
            pltpu.VMEM((8, 64, 256), BF),
            pltpu.VMEM((640, 512), F32),
            dma((16, 2)), dma((2,)),
            dma((8,)), dma((8,)), dma((2, 4)), dma((2, 4)), dma((4, 8)), dma((4, 8)),
            dma((4, 8)), dma((4, 8)), dma((8,)), dma((8,)),
            dma((2, 8)), dma((2, 8)), dma((4, 8)), dma((4, 8)), dma((4, 8)), dma((4, 8)),
            dma((2, 4, 8)), dma((2, 4, 8)), dma((8,)), dma((8,)),
        ],
        compiler_params=pltpu.CompilerParams(
            collective_id=0, has_side_effects=True, vmem_limit_bytes=56 << 20
        ),
        cost_estimate=pl.CostEstimate(
            flops=4 * steps * rows * width * 512, bytes_accessed=12 << 20, transcendentals=0
        ),
        name="project_and_reduce",
    )(activations, cotangent, piece)
    grad = grad.T
    new_first = 0.9 * first_moment + 0.1 * grad
    new_second = 0.95 * second_moment + 0.05 * grad * grad
    mhat = new_first / (1.0 - 0.9**10)
    vhat = new_second / (1.0 - 0.95**10)
    new_master = master - 0.0003 * (mhat / (jnp.sqrt(vhat) + 1e-08) + 0.1 * master)
    return (keys, new_master, new_first, new_second)


def solution(mesh):
    placed = (
        P(None, ("node", "local"), None),
        P(None, ("node", "local"), None),
        P("node", "local"),
        P("node", "local"),
        P("node", "local"),
    )
    return jax.shard_map(
        per_device,
        mesh=mesh,
        in_specs=placed,
        out_specs=(
            P(None, ("node", "local"), None),
            P("node", "local"),
            P("node", "local"),
            P("node", "local"),
        ),
        check_vma=False,
    )
```

time: 598 us -> 81.8 us (0.14)
  waiting for transfers between devices: 539 us -> 0 us
  Pallas kernels: 0 us -> 75.9 us
  matrix products: 26 us -> 0 us
  between operations: 13.8 us -> 0.66 us
  local copies, waits for them, and re-layouts: 13 us -> 1.98 us
    all_gather x2 -> x0, waiting for transfers between devices: 248 us -> none  [the longest x1 170 us: per_device(): lax.all_gather(secondary, 'local', axis=1, tiled=True)]
    unnamed x5 -> x0, waiting for transfers between devices: 176 us -> none
    reduce_scatter x1 -> x0, waiting for transfers between devices: 115 us -> none  [per_device(): lax.psum_scatter(partial_sum, 'node', scatter_dimension=0, tiled=True)]
    pallas_call x0 -> x1, Pallas kernels: none -> 75.9 us  [per_device(): pl.pallas_call(functools.partial(kernel, gscale), out_shape=(jax.ShapeDty...]
    dot_general x3 -> x0, matrix products: 26 us -> none  [the longest x1 13.1 us: per_device(): lax.dot_general(activations, cotangent, (((0, 1), (0, 1)), ((), ())), pre...]
    unnamed x11 -> x7, local copies, waits for them, and re-layouts: 13 us -> 1.98 us
  transfers between devices with their start and end apart: 4 -> 0, of which waited for: 4 -> 0; matrix products, arithmetic and copies ran while one was open for 0% -> 0% of each run, Pallas kernels for 0% -> 0%
where the time goes in v1:
time: 81.8 us; the launch traced here: 81.5 us
  Pallas kernels  75.9 us (93%)
  other arithmetic  3 us (4%)
  local copies, waits for them, and re-layouts  1.98 us (2%)
    pallas_call x1, Pallas kernels, per_device(): pl.pallas_call(functools.partial(kernel, gscale), out_shape=(jax.ShapeDty...  75.9 us
    unnamed x7, local copies, waits for them, and re-layouts  1.98 us

profile of v1, /device:TPU:1, one launch (start us, length us, event | category | flops | bytes accessed | tf_op | source)
XLA Modules:
  0.0 81.5 jit_solution(9108183575266834595)
XLA Ops:
  0.6 1.5 %convert_bitcast_fusion.w_ref = bf16[64,256]{1,0:T(8,128)(2,1)} fusion(f32[256,64]{0,1:T(8,128)} %param.7), kind=kLoop, calls=%fused_computation.5 | loop fusion | flops 16384 | bytes 98304 | tf_op jit(solution)/shard_map/transpose | solution.py:343
  2.1 0.0 copy-start
  2.1 0.0 copy-start.1
  2.1 0.0 copy-start.2
  2.1 75.9 %project_and_reduce.1 = (bf16[2,320,512]{2,1,0:T(8,128)(2,1)}, f32[64,256]{1,0:T(8,128)}) custom-call(bf16[2,320,8192]{2,1,0:T(8,128)(2,1)} %a_hbm.1, bf16[2,320,512]{2,1,0:T(8,128)(2,1)} %c_hbm.1, bf16[64,256]{1,0:T(8,128)(2,1)} %convert_bitcast_fusion.w_ref), custom_call_target="tpu_custom_call" | custom-call | flops 10737418240 | bytes 12582912 | tf_op jit(solution)/shard_map/project_and_reduce/pallas_call | solution.py:347
  78.0 0.0 copy-done
  78.0 0.0 copy-done.1
  78.0 0.0 copy-done.2
  78.0 1.5 %multiply_subtract_fusion = (f32[256,64]{0,1:T(8,128)}, f32[256,64]{0,1:T(8,128)}, f32[256,64]{0,1:T(8,128)}) fusion(f32[256,64]{0,1:T(8,128)S(1)} %copy-done, f32[64,256]{1,0:T(8,128)} %get-tuple-element.7, f32[256,64]{0,1:T(8,128)S(1)} %copy-done.1, f32[256,64]{0,1:T(8,128)S(1)} %copy-done.2), kind=kLoop, calls=%fused_computation.4 | loop fusion | flops 245760 | bytes 458752 | tf_op jit(solution)/shard_map/sub | solution.py:389
  79.6 2.0 %copy.10 = bf16[2,320,512]{2,1,0:T(8,128)(2,1)} copy(bf16[2,320,512]{2,1,0:T(8,128)(2,1)} %get-tuple-element.15) | data formatting | bytes 1310720
Async XLA Ops:
  2.1 75.9 %copy-start = (f32[256,64]{0,1:T(8,128)S(1)}, f32[256,64]{0,1:T(8,128)}, u32[]{:S(2)}) copy-start(f32[256,64]{0,1:T(8,128)} %param.7) | copy-start | bytes 196612
  2.1 75.9 %copy-start.1 = (f32[256,64]{0,1:T(8,128)S(1)}, f32[256,64]{0,1:T(8,128)}, u32[]{:S(2)}) copy-start(f32[256,64]{0,1:T(8,128)} %param.8) | copy-start | bytes 196612
  2.1 75.9 %copy-start.2 = (f32[256,64]{0,1:T(8,128)S(1)}, f32[256,64]{0,1:T(8,128)}, u32[]{:S(2)}) copy-start(f32[256,64]{0,1:T(8,128)} %param.9) | copy-start | bytes 196612

commit v2 on v1

v2 whole, which is shorter than its diff:
```python
import functools
import math

import jax
import jax.numpy as jnp
from jax import lax
from jax.experimental import pallas as pl
from jax.experimental.pallas import tpu as pltpu
from jax.sharding import PartitionSpec as P

BF = jnp.bfloat16
F32 = jnp.float32
MESH = pl.DeviceIdType.MESH

ORDER = "".join((
    "T0T1G1V0G2P0R0G4H0G3P1T2H1G5G6W0B0H2G7R1H4J0P2R2",
    "H3B1T3J1T4H6H5U2P3J2U1T5H7J4T6B2R3P4R4J3P5P6U3U4",
    "T7J6C0J5B3C1P7S0J7S1S2R5S4R6C2B4S3K0U5B6U6B5S5D0",
    "S6K1D1B7C3R7D2C4K2U7C6S7C5K3C7D3K4D4L0D6D5D7",
))

GROUPS = ((0, 1), (2, 3), (4, 5), (6,), (7,))
AHEAD = 2


def device_of(x, y, z, c):
    return ((y // 2) * 16 + z * 2 + c, x * 2 + y % 2)


def kernel(gscale, a_hbm, c_hbm, w_ref, keys_ref, grad_ref,
           a, cb, ct, mb, wt, g, rsib, r1ax, r1bx, r1ay, r1by, r2x, r2y, r3x, r3y, rz, rzb, rz2, rzb2, rz3, rzb3, acc,
           sem_a, sem_c, sem_m,
           ag1s, ag1r, ag2s, ag2r, agas, agar, agbs, agbr, agcs, agcr,
           z1s, z1r, z2s, z2r, zrs, zrr,
           sibs, sibr, rsas, rsar, rsbs, rsbr, rs2s, rs2r, rs3s, rs3r,
           szs, szr, sz2s, sz2r, sz3s, sz3r):
    node, local = lax.axis_index("node"), lax.axis_index("local")
    c, z, yh = node % 2, (node // 2) % 8, node // 16
    x, yl = local // 2, local % 2
    y = yh * 2 + yl
    lo, hi = pl.ds(0, 128), pl.ds(128, 128)
    upper, mid, top, low = pl.ds(0, 32), pl.ds(32, 16), pl.ds(0, 48), pl.ds(48, 16)

    def at_x(d):
        return device_of((x + d) % 4, y, z, c)

    def at_y(d):
        return device_of(x, (y + d) % 4, z, c)

    def at_z(d):
        return device_of(x, y, (z + d) % 8, c)

    sibling = device_of(x, y, z, 1 - c)

    def send(src, dst, ss, rs, device):
        return pltpu.make_async_remote_copy(
            src_ref=src, dst_ref=dst, send_sem=ss, recv_sem=rs, device_id=device, device_id_type=MESH
        )

    def arrived(ref, sem):
        pltpu.make_async_copy(ref, ref, sem).wait()

    def pieces(n):
        for per, rest in (
            (16, ()), (8, (0,)), (6, (0, pl.ds(0, 3))), (4, (0, slice(None), 0)),
            (3, (0, pl.ds(0, 3), 0)), (2, (0, 0)), (1, (0, 0, 0)),
        ):
            if n % per == 0 and n // per <= 8:
                return wt.at[(0, pl.ds(0, n // per), *rest)]

    def far_first(i):
        return (z + (4 - (i + 1) // 2 if i % 2 == 1 else 4 + i // 2)) % 8

    def near_first(i):
        return far_first(7 - i)

    barrier = pltpu.get_barrier_semaphore()
    partners = [at_x(d) for d in (1, 2, 3)] + [at_y(d) for d in (1, 2, 3)]
    partners += [at_z(d) for d in range(1, 8)] + [sibling]
    for device in partners:
        pl.semaphore_signal(barrier, inc=1, device_id=device, device_id_type=MESH)

    def load_c(m):
        return pltpu.make_async_copy(c_hbm.at[m], cb.at[pl.ds(320 * m, 320)], sem_c)

    def load_a(zz, h, m):
        block = h * 8 + zz
        return pltpu.make_async_copy(
            a_hbm.at[m, :, pl.ds(pl.multiple_of(block * 512, 512), 512)],
            a.at[block, pl.ds(320 * m, 320)],
            sem_a.at[zz],
        )

    def load_slice(i):
        zz = far_first(i)
        for h in range(2):
            for m in range(2):
                load_a(zz, h, m).start()

    load_m = pltpu.make_async_copy(w_ref, mb, sem_m)
    load_m.start()
    for m in range(2):
        load_c(m).start()
    for i in range(AHEAD):
        load_slice(i)

    def ag1(d):
        piece = wt.at[yh, z, c, x, yl, top]
        return send(piece, piece, ag1s, ag1r.at[d], at_z(d))

    def agz1(d):
        piece = wt.at[yh, z, c, x, yl, low]
        return send(piece, piece, z1s, z1r, at_y(d))

    def agz2(d):
        piece = wt.at[:, z, c, x, :, low]
        return send(piece, piece, z2s, z2r, at_x(d))

    def ring_send(zz, k, up):
        piece = wt.at[:, zz, c, :, :, low]
        if up:
            return send(piece, piece, zrs, zrr.at[0, k], at_z(1))
        return send(piece, piece, zrs, zrr.at[1, k], at_z(7))

    def ring_half(up):
        if up:
            piece = wt.at[0, (z + 5) % 8, c, :, :, low]
            return send(piece, piece, zrs, zrr.at[0, 4], at_z(1))
        piece = wt.at[1, (z + 3) % 8, c, :, :, low]
        return send(piece, piece, zrs, zrr.at[1, 4], at_z(7))

    def ag2(zz, d):
        left = wt.at[yh, zz, c, x, yl, top, lo]
        right = wt.at[yh, zz, c, x, yl, top, hi]
        return (
            send(left, left, ag2s, ag2r.at[zz], at_y(d)),
            send(right, right, ag2s, ag2r.at[zz], at_x(d)),
        )

    def ag_second(i):
        zz = near_first(i)

        @pl.when(i > 0)
        def _():
            ag1((z - zz + 8) % 8).wait_recv()

        for d in (1, 3, 2):
            for copy in ag2(zz, d):
                copy.start()

    def ag_low_second(_):
        arrived(rz3, z1r)
        for d in (1, 3, 2):
            agz2(d).start()

    def ag_low_third(_):
        arrived(rz2, z2r)
        ring_send(z, 1, True).start()
        ring_send(z, 1, False).start()

    def ag_ring(i):
        k = (i + 1) // 2

        @pl.when((i < 7) & (i % 2 == 1))
        def _():
            ring_send(z, k, True).wait_recv()
            pl.when(k < 3)(lambda: ring_send((z - k + 8) % 8, k + 1, True).start())
            pl.when(k == 3)(lambda: ring_half(True).start())

        @pl.when((i > 0) & (i % 2 == 0))
        def _():
            ring_send(z, k, False).wait_recv()
            pl.when(k < 3)(lambda: ring_send((z + k) % 8, k + 1, False).start())
            pl.when(k == 3)(lambda: ring_half(False).start())

        @pl.when(i == 7)
        def _():
            ring_half(True).wait_recv()
            ring_half(False).wait_recv()

    def aga(zz):
        left = wt.at[:, zz, c, x, :, top, lo]
        right = wt.at[yh, zz, c, :, yl, top, hi]
        return (
            send(left, left, agas, agar.at[zz], at_x(1)),
            send(left, left, agas, agar.at[zz], at_x(3)),
            send(right, right, agas, agar.at[zz], at_y(1)),
            send(right, right, agas, agar.at[zz], at_y(3)),
        )

    def agb(zz):
        before, after = (x + 3) % 4, (x + 1) % 4
        below, above = (y + 3) % 4, (y + 1) % 4
        parts = (
            wt.at[0, zz, c, before, :, top, lo],
            wt.at[1, zz, c, after, :, top, lo],
            wt.at[below // 2, zz, c, pl.ds(0, 2), below % 2, top, hi],
            wt.at[above // 2, zz, c, pl.ds(2, 2), above % 2, top, hi],
        )
        to = (at_x(1), at_x(3), at_y(1), at_y(3))
        return tuple(
            send(parts[k], parts[k], agbs, agbr.at[zz], to[k]) for k in range(4)
        )

    def agc(zz):
        part = wt.at[:, zz, c]
        return send(part, part, agcs, agcr.at[zz], sibling)

    def sib(zz, h):
        return send(
            g.at[h, zz, 1 - c], rsib.at[h, zz], sibs, sibr.at[zz], sibling
        )

    def rs_terms(i):
        zz = far_first(i)
        arrived(a.at[pl.ds(0, 2)], sem_a.at[zz])
        if i + AHEAD < 8:
            load_slice(i + AHEAD)
        rows = jnp.concatenate([a[zz], a[8 + zz]], axis=1)
        for half in range(2):
            total = jnp.dot(
                ct[256 * half : 256 * half + 256, :], rows, preferred_element_type=F32
            )
            term = (total * gscale).astype(BF)
            for h in range(2):
                for q in range(2):
                    col = 512 * h + 256 * q
                    g[h, zz, q, 2 * half : 2 * half + 2] = term[:, col : col + 256].reshape(2, 2, 64, 256)
        for h in range(2):
            sib(zz, h).start()

    def add(*terms):
        total = terms[0].astype(F32)
        for term in terms[1:]:
            total = total + term.astype(F32)
        return total.astype(BF)

    def rsa(zz):
        far_x = (x + 2) % 4
        return (
            send(g.at[0, zz, c, far_x, :, upper, lo], r1ax.at[0, zz], rsas, rsar.at[zz], at_x(1)),
            send(g.at[1, zz, c, far_x, :, upper, lo], r1ax.at[1, zz], rsas, rsar.at[zz], at_x(3)),
            send(g.at[1 - yh, zz, c, pl.ds(0, 2), yl, top, hi], r1ay.at[0, zz], rsas,
                 rsar.at[zz], at_y(1)),
            send(g.at[1 - yh, zz, c, pl.ds(2, 2), yl, top, hi], r1ay.at[1, zz], rsas,
                 rsar.at[zz], at_y(3)),
        )

    def rs_pair(i):
        zz = far_first(i)
        arrived(rsib.at[:, zz], sibr.at[zz])
        for h in range(2):

            @pl.loop(0, 4)
            def _(k):
                g[h, zz, c, k] = add(g[h, zz, c, k], rsib[h, zz, k])

        for copy in rsa(zz):
            copy.start()

    def rsb(zz):
        before, after = (x + 3) % 4, (x + 1) % 4
        below, above = (y + 3) % 4, (y + 1) % 4
        return (
            send(g.at[:, zz, c, after, :, upper, lo], r1bx.at[0, zz], rsbs, rsbr.at[zz], at_x(1)),
            send(g.at[:, zz, c, before, :, upper, lo], r1bx.at[1, zz], rsbs, rsbr.at[zz], at_x(3)),
            send(g.at[above // 2, zz, c, :, above % 2, top, hi], r1by.at[0, zz], rsbs,
                 rsbr.at[zz], at_y(1)),
            send(g.at[below // 2, zz, c, :, below % 2, top, hi], r1by.at[1, zz], rsbs,
                 rsbr.at[zz], at_y(3)),
        )

    def rs_pass(i):
        zz = far_first(i)
        before, after = (x + 3) % 4, (x + 1) % 4
        below, above = (y + 3) % 4, (y + 1) % 4
        arrived(r1ax.at[0, pl.ds(0, 5)], rsar.at[zz])
        g[0, zz, c, after, :, upper, lo] = add(g[0, zz, c, after, :, upper, lo], r1ax[0, zz])
        g[1, zz, c, before, :, upper, lo] = add(g[1, zz, c, before, :, upper, lo], r1ax[1, zz])
        for k in range(2):
            g[above // 2, zz, c, k, above % 2, top, hi] = add(
                g[above // 2, zz, c, k, above % 2, top, hi], r1ay[0, zz, k]
            )
            g[below // 2, zz, c, 2 + k, below % 2, top, hi] = add(
                g[below // 2, zz, c, 2 + k, below % 2, top, hi], r1ay[1, zz, k]
            )
        for copy in rsb(zz):
            copy.start()

    def rs2(zz, d):
        to_y, to_x = (y + d) % 4, (x + d) % 4
        return (
            send(g.at[to_y // 2, zz, c, x, to_y % 2, upper, lo], r2x.at[d - 1, zz], rs2s,
                 rs2r.at[zz], at_y(d)),
            send(g.at[yh, zz, c, to_x, yl, top, hi], r2y.at[d - 1, zz], rs2s,
                 rs2r.at[zz], at_x(d)),
        )

    def rs_second(i):
        zz = far_first(i)
        arrived(r1bx.at[0, pl.ds(0, 5)], rsbr.at[zz])
        for h in range(2):
            for k in range(2):
                g[h, zz, c, x, k, upper, lo] = add(
                    g[h, zz, c, x, k, upper, lo], r1bx[0, zz, h, k], r1bx[1, zz, h, k]
                )
        for k in range(4):
            g[yh, zz, c, k, yl, top, hi] = add(g[yh, zz, c, k, yl, top, hi], r1by[0, zz, k], r1by[1, zz, k])
        for d in (1, 3, 2):
            for copy in rs2(zz, d):
                copy.start()

    def rs3(zz, d):
        own, to = g.at[yh, zz, c, x, yl], device_of(x, y, zz, c)
        return (
            send(own.at[upper, lo], r3x.at[d], rs3s.at[0], rs3r.at[0], to),
            send(own.at[top, hi], r3y.at[d], rs3s.at[1], rs3r.at[1], to),
        )

    def rs_third(i):
        zz = far_first(i)
        arrived(r1by.at[0, pl.ds(0, 5), 0], rs2r.at[zz])
        g[yh, zz, c, x, yl, upper, lo] = add(
            g[yh, zz, c, x, yl, upper, lo], r2x[0, zz], r2x[1, zz], r2x[2, zz]
        )
        g[yh, zz, c, x, yl, top, hi] = add(
            g[yh, zz, c, x, yl, top, hi], r2y[0, zz], r2y[1, zz], r2y[2, zz]
        )

        @pl.when(i < 7)
        def _():
            for copy in rs3(zz, (zz - z + 8) % 8):
                copy.start()

    def rz_send(zz, k, up):
        q = 0 if up else 1
        to = at_z(1) if up else at_z(7)
        return (
            send(g.at[:, zz, c, :, :, low], rz.at[q, k], szs, szr.at[q, k], to),
            send(g.at[:, zz, c, :, :, mid, lo], rzb.at[q, k], szs, szr.at[q, k], to),
        )

    def rz_half(up):
        zz = (z + 4) % 8
        q = 0 if up else 1
        to = at_z(1) if up else at_z(7)
        return (
            send(g.at[q, zz, c, :, :, low], rz.at[q, 4, q], szs, szr.at[q, 4], to),
            send(g.at[q, zz, c, :, :, mid, lo], rzb.at[q, 4, q], szs, szr.at[q, 4], to),
        )

    def start(copies):
        for copy in copies:
            copy.start()

    def rz_arrived(up, k):
        arrived(pieces(3 if k == 4 else 6), szr.at[0 if up else 1, k])

    def rz_add(zz, h, q, k):
        for e in range(4):
            g[h, zz, c, e, :, low] = add(g[h, zz, c, e, :, low], rz[q, k, h, e])
            g[h, zz, c, e, :, mid, lo] = add(g[h, zz, c, e, :, mid, lo], rzb[q, k, h, e])

    def rs_ring(i):
        zz = far_first(i)
        k = 4 - (i + 1) // 2
        j = 4 - i // 2

        @pl.when(i == 0)
        def _():
            start(rz_half(True))
            start(rz_half(False))

        @pl.when((i % 2 == 1) & (i < 7))
        def _():
            @pl.when(k == 3)
            def _():
                rz_arrived(True, 4)
                rz_add(zz, 0, 0, 4)

            @pl.when(k < 3)
            def _():
                rz_arrived(True, k + 1)
                rz_add(zz, 0, 0, k + 1)
                rz_add(zz, 1, 0, k + 1)

            start(rz_send(zz, k, True))

        @pl.when((i % 2 == 0) & (i > 0))
        def _():
            @pl.when(j == 3)
            def _():
                rz_arrived(False, 4)
                rz_add(zz, 1, 1, 4)

            @pl.when(j < 3)
            def _():
                rz_arrived(False, j + 1)
                rz_add(zz, 0, 1, j + 1)
                rz_add(zz, 1, 1, j + 1)

            start(rz_send(zz, j, False))

        @pl.when(i == 7)
        def _():
            for q in range(2):
                rz_arrived(q == 0, 1)
                rz_add(z, 0, q, 1)
                rz_add(z, 1, q, 1)
            for d in (1, 3, 2):
                start(rz_second(d))

    def rz_second(d):
        to_x = (x + d) % 4
        return (
            send(g.at[:, z, c, to_x, :, low], rz2.at[d - 1], sz2s, sz2r, at_x(d)),
            send(g.at[:, z, c, to_x, :, mid, lo], rzb2.at[d - 1], sz2s, sz2r, at_x(d)),
        )

    def rz_third(d):
        to_y = (y + d) % 4
        part = g.at[to_y // 2, z, c, x, to_y % 2]
        return (
            send(part.at[low], rz3.at[d - 1], sz3s, sz3r, at_y(d)),
            send(part.at[mid, lo], rzb3.at[d - 1], sz3s, sz3r, at_y(d)),
        )

    def rz_last(_):
        arrived(r1by.at[0, pl.ds(0, 3)], sz2r)
        for h in range(2):
            for k in range(2):
                g[h, z, c, x, k, low] = add(
                    g[h, z, c, x, k, low], rz2[0, h, k], rz2[1, h, k], rz2[2, h, k]
                )
                g[h, z, c, x, k, mid, lo] = add(
                    g[h, z, c, x, k, mid, lo], rzb2[0, h, k], rzb2[1, h, k], rzb2[2, h, k]
                )
        for d in (1, 3, 2):
            start(rz_third(d))

    def project(group):
        slices = [near_first(i) for i in GROUPS[group]]
        for zz in slices:
            agc(zz).wait_recv()
        blocks = [(h, zz) for zz in slices for h in range(2)]
        rows = jnp.concatenate([a[h * 8 + zz] for h, zz in blocks], axis=1)
        piece = jnp.concatenate(
            [wt[h, zz, q].reshape(512, 256) for h, zz in blocks for q in range(2)], axis=1
        )
        total = lax.dot_general(rows, piece, (((1,), (1,)), ((), ())), preferred_element_type=F32)
        if group > 0:
            total = acc[...] + total
        if group < len(GROUPS) - 1:
            acc[...] = total
        else:
            keys_ref[...] = total.astype(BF).reshape(2, 320, 512)

    def ag_a(i):
        zz = near_first(i)
        arrived(r2y.at[:, pl.ds(0, 2)], ag2r.at[zz])
        for copy in aga(zz):
            copy.start()

    def ag_b(i):
        zz = near_first(i)
        arrived(r1ay.at[0], agar.at[zz])
        for copy in agb(zz):
            copy.start()

    def ag_c(i):
        zz = near_first(i)
        arrived(r1ay.at[0, pl.ds(0, 4)], agbr.at[zz])
        agc(zz).start()

    load_m.wait()
    wt[yh, z, c, x, yl] = mb[...].astype(BF)
    arrived(cb, sem_c)
    ct[...] = cb[...].T
    pl.semaphore_wait(barrier, len(partners))
    for d in (1, 3, 2):
        agz1(d).start()
    for d in (1, 7, 2, 6, 3, 5, 4):
        ag1(d).start()
    ag_second(0)

    stages = dict(
        T=rs_terms, P=rs_pair, R=rs_ring, B=rs_pass, C=rs_second, D=rs_third, L=rz_last,
        G=ag_second, V=ag_low_second, W=ag_low_third, H=ag_a, J=ag_b, U=ag_ring, S=ag_c, K=project,
    )
    for letter, digit in zip(ORDER[::2], ORDER[1::2]):
        stages[letter](int(digit))

    def total(rows, columns, terms):
        value = g[yh, z, c, x, yl, rows, columns].astype(F32)
        for term in terms:
            value = value + term.astype(F32)
        grad_ref[rows, columns] = value

    arrived(r3x.at[pl.ds(1, 7)], rs3r.at[0])
    arrived(r3y.at[pl.ds(1, 7)], rs3r.at[1])
    total(upper, lo, [r3x[d] for d in range(1, 8)])
    total(top, hi, [r3y[d] for d in range(1, 8)])
    arrived(r1by.at[0, 0, pl.ds(0, 3)], sz3r)
    total(low, pl.ds(0, 256), [rz3[k] for k in range(3)])
    total(mid, lo, [rzb3[k] for k in range(3)])

    for ref, sem in (
        (r1by.at[0, pl.ds(0, 7), pl.ds(0, 2)], ag1s), (rz3, z1s), (rz2, z2s), (pieces(28), zrs),
        (pieces(18), ag2s), (pieces(48), agas), (pieces(24), agbs), (rsib, agcs),
        (rsib, sibs), (pieces(20), rsas), (pieces(40), rsbs), (pieces(15), rs2s),
        (r3x.at[pl.ds(1, 7)], rs3s.at[0]), (r3y.at[pl.ds(1, 7)], rs3s.at[1]), (pieces(42), szs),
        (r1by.at[0, pl.ds(0, 3)], sz2s), (r1by.at[0, 0, pl.ds(0, 3)], sz3s),
    ):
        arrived(ref, sem)


def update(keys_ref, grad_ref, master_ref, first_ref, second_ref,
           keys_out, master_out, first_out, second_out):
    keys_out[...] = keys_ref[...]
    grad, master = grad_ref[...], master_ref[...]
    new_first = 0.9 * first_ref[...] + 0.1 * grad
    new_second = 0.95 * second_ref[...] + 0.05 * grad * grad
    mhat = new_first / (1.0 - 0.9**10)
    vhat = new_second / (1.0 - 0.95**10)
    first_out[...] = new_first
    second_out[...] = new_second
    master_out[...] = master - 0.0003 * (mhat / (jnp.sqrt(vhat) + 1e-08) + 0.1 * master)


def per_device(activations, cotangent, master, first_moment, second_moment):
    steps, rows, width = activations.shape
    gscale = 1.0 / math.sqrt(steps * rows * lax.axis_size("node") * lax.axis_size("local"))
    any_spec = pl.BlockSpec(memory_space=pl.ANY)
    vmem = pl.BlockSpec(memory_space=pltpu.VMEM)
    dma = pltpu.SemaphoreType.DMA
    keys, grad = pl.pallas_call(
        functools.partial(kernel, gscale),
        out_shape=(
            jax.ShapeDtypeStruct((2, 320, 512), BF),
            jax.ShapeDtypeStruct((64, 256), F32),
        ),
        in_specs=[any_spec, any_spec, any_spec],
        out_specs=(vmem, vmem),
        scratch_shapes=[
            pltpu.VMEM((16, 640, 512), BF),
            pltpu.VMEM((640, 512), BF),
            pltpu.VMEM((512, 640), BF),
            pltpu.VMEM((64, 256), F32),
            pltpu.VMEM((2, 8, 2, 4, 2, 64, 256), BF),
            pltpu.VMEM((2, 8, 2, 4, 2, 64, 256), BF),
            pltpu.VMEM((2, 8, 4, 2, 64, 256), BF),
            pltpu.VMEM((2, 8, 2, 32, 128), BF),
            pltpu.VMEM((2, 8, 2, 2, 32, 128), BF),
            pltpu.VMEM((2, 8, 2, 48, 128), BF),
            pltpu.VMEM((2, 8, 4, 48, 128), BF),
            pltpu.VMEM((3, 8, 32, 128), BF),
            pltpu.VMEM((3, 8, 48, 128), BF),
            pltpu.VMEM((8, 32, 128), BF),
            pltpu.VMEM((8, 48, 128), BF),
            pltpu.VMEM((2, 5, 2, 4, 2, 16, 256), BF),
            pltpu.VMEM((2, 5, 2, 4, 2, 16, 128), BF),
            pltpu.VMEM((3, 2, 2, 16, 256), BF),
            pltpu.VMEM((3, 2, 2, 16, 128), BF),
            pltpu.VMEM((3, 16, 256), BF),
            pltpu.VMEM((3, 16, 128), BF),
            pltpu.VMEM((640, 512), F32),
            dma((8,)), dma, dma,
            dma, dma((8,)), dma, dma((8,)), dma, dma((8,)),
            dma, dma((8,)), dma, dma((8,)),
            dma, dma, dma, dma, dma, dma((2, 5)),
            dma, dma((8,)), dma, dma((8,)), dma, dma((8,)),
            dma, dma((8,)), dma((2,)), dma((2,)),
            dma, dma((2, 5)), dma, dma, dma, dma,
        ],
        compiler_params=pltpu.CompilerParams(
            collective_id=0, has_side_effects=True, vmem_limit_bytes=56 << 20
        ),
        cost_estimate=pl.CostEstimate(
            flops=4 * steps * rows * width * 512, bytes_accessed=12 << 20, transcendentals=0
        ),
        name="project_and_reduce",
    )(activations, cotangent, master.T)
    keys, new_master, new_first, new_second = pl.pallas_call(
        update,
        out_shape=(jax.ShapeDtypeStruct((2, 320, 512), BF),) + (jax.ShapeDtypeStruct((64, 256), F32),) * 3,
        in_specs=[vmem] * 5,
        out_specs=(vmem,) * 4,
        name="adam_update",
    )(keys, grad, master.T, first_moment.T, second_moment.T)
    return (keys, new_master.T, new_first.T, new_second.T)


def solution(mesh):
    placed = (
        P(None, ("node", "local"), None),
        P(None, ("node", "local"), None),
        P("node", "local"),
        P("node", "local"),
        P("node", "local"),
    )
    return jax.shard_map(
        per_device,
        mesh=mesh,
        in_specs=placed,
        out_specs=(
            P(None, ("node", "local"), None),
            P("node", "local"),
            P("node", "local"),
            P("node", "local"),
        ),
        check_vma=False,
    )
```

time: 81.8 us -> 56.2 us (0.69)
  Pallas kernels: 75.9 us -> 55.3 us
  other arithmetic: 3 us -> 0 us
  local copies, waits for them, and re-layouts: 1.98 us -> 0 us
    pallas_call x1, Pallas kernels: 75.9 us -> 53.2 us  [per_device(): pl.pallas_call(functools.partial(kernel, gscale), out_shape=(jax.ShapeDty...]
    pallas_call x0 -> x1, Pallas kernels: none -> 2.12 us  [per_device(): pl.pallas_call(update, out_shape=(jax.ShapeDtypeStruct((2, 320, 512), BF)...]
    unnamed x7 -> x0, local copies, waits for them, and re-layouts: 1.98 us -> none
    sub x1 -> x0, other arithmetic: 1.54 us -> none  [per_device(): master - 0.0003 * (mhat / (jnp.sqrt(vhat) + 1e-08) + 0.1 * master)]
    transpose x1 -> x0, other arithmetic: 1.46 us -> none  [per_device(): piece = master.astype(BF).T]
where the time goes in v2:
time: 56.2 us; the launch traced here: 56 us
  Pallas kernels  55.3 us (98%)
  between operations  0.64 us (1%)
    pallas_call x1, Pallas kernels, per_device(): pl.pallas_call(functools.partial(kernel, gscale), out_shape=(jax.ShapeDty...  53.2 us
    pallas_call x1, Pallas kernels, per_device(): pl.pallas_call(update, out_shape=(jax.ShapeDtypeStruct((2, 320, 512), BF)...  2.12 us

profile of v2, /device:TPU:1, one launch (start us, length us, event | category | flops | bytes accessed | tf_op | source)
XLA Modules:
  0.0 56.0 jit_solution(9748177851074771730)
XLA Ops:
  0.6 53.2 %project_and_reduce.1 = (bf16[2,320,512]{2,1,0:T(8,128)(2,1)}, f32[64,256]{1,0:T(8,128)}) custom-call(bf16[2,320,8192]{2,1,0:T(8,128)(2,1)} %a_hbm.1, bf16[2,320,512]{2,1,0:T(8,128)(2,1)} %c_hbm.1, f32[64,256]{1,0:T(8,128)} %bitcast.6), custom_call_target="tpu_custom_call" | custom-call | flops 10737418240 | bytes 12582912 | tf_op jit(solution)/shard_map/project_and_reduce/pallas_call | solution.py:536
  53.8 2.1 %adam_update.1 = (bf16[2,320,512]{2,1,0:T(8,128)(2,1)}, f32[64,256]{1,0:T(8,128)}, f32[64,256]{1,0:T(8,128)}, f32[64,256]{1,0:T(8,128)}) custom-call(bf16[2,320,512]{2,1,0:T(8,128)(2,1)} %get-tuple-element.10.keys_ref, f32[64,256]{1,0:T(8,128)} %get-tuple-element.11.grad_ref, f32[64,256]{1,0:T(8,128)} %bitcast.7, f32[64,256]{1,0:T(8,128)} %bitcast.8, ...), custom_call_target="tpu_custom_call" | custom-call | tf_op jit(solution)/shard_map/adam_update/pallas_call | solution.py:583

commit v3 on v2

--- a/solution.py
+++ b/solution.py
@@ -16,10 +16,10 @@
     "T0T1G1V0G2P0R0G4H0G3P1T2H1G5G6W0B0H2G7R1H4J0P2R2",
     "H3B1T3J1T4H6H5U2P3J2U1T5H7J4T6B2R3P4R4J3P5P6U3U4",
     "T7J6C0J5B3C1P7S0J7S1S2R5S4R6C2B4S3K0U5B6U6B5S5D0",
-    "S6K1D1B7C3R7D2C4K2U7C6S7C5K3C7D3K4D4L0D6D5D7",
+    "S6K1D1B7C3R7D2C4K2U7C6S7C5K3C7X0D3Y0D4L0D6D5D7",
 ))
 
-GROUPS = ((0, 1), (2, 3), (4, 5), (6,), (7,))
+GROUPS = ((0, 1), (2, 3), (4, 5), (6,))
 AHEAD = 2
 
 
@@ -29,7 +29,7 @@
 
 def kernel(gscale, a_hbm, c_hbm, w_ref, keys_ref, grad_ref,
            a, cb, ct, mb, wt, g, rsib, r1ax, r1bx, r1ay, r1by, r2x, r2y, r3x, r3y, rz, rzb, rz2, rzb2, rz3, rzb3, acc,
-           sem_a, sem_c, sem_m,
+           keys, sem_a, sem_c, sem_m, sem_k,
            ag1s, ag1r, ag2s, ag2r, agas, agar, agbs, agbr, agcs, agcr,
            z1s, z1r, z2s, z2r, zrs, zrr,
            sibs, sibr, rsas, rsar, rsbs, rsbr, rs2s, rs2r, rs3s, rs3r,
@@ -448,12 +448,27 @@
             [wt[h, zz, q].reshape(512, 256) for h, zz in blocks for q in range(2)], axis=1
         )
         total = lax.dot_general(rows, piece, (((1,), (1,)), ((), ())), preferred_element_type=F32)
-        if group > 0:
-            total = acc[...] + total
-        if group < len(GROUPS) - 1:
-            acc[...] = total
-        else:
-            keys_ref[...] = total.astype(BF).reshape(2, 320, 512)
+        acc[...] = acc[...] + total if group > 0 else total
+
+    def project_last(core):
+        zz = near_first(7)
+        columns = pl.ds(pl.multiple_of(core * 256, 256), 256)
+        rows = jnp.concatenate([a[zz, :, columns], a[8 + zz, :, columns]], axis=1)
+        piece = jnp.concatenate([wt[h, zz, core].reshape(512, 256) for h in range(2)], axis=1)
+        return acc[...] + lax.dot_general(
+            rows, piece, (((1,), (1,)), ((), ())), preferred_element_type=F32
+        )
+
+    def project_own(_):
+        acc[...] = project_last(c)
+
+    def store_keys():
+        return pltpu.make_async_copy(keys, keys_ref, sem_k)
+
+    def project_sibling(_):
+        agc(near_first(7)).wait_recv()
+        keys[...] = project_last(1 - c).astype(BF).reshape(2, 320, 512)
+        store_keys().start()
 
     def ag_a(i):
         zz = near_first(i)
@@ -485,7 +500,7 @@
 
     stages = dict(
         T=rs_terms, P=rs_pair, R=rs_ring, B=rs_pass, C=rs_second, D=rs_third, L=rz_last,
-        G=ag_second, V=ag_low_second, W=ag_low_third, H=ag_a, J=ag_b, U=ag_ring, S=ag_c, K=project,
+        G=ag_second, V=ag_low_second, W=ag_low_third, H=ag_a, J=ag_b, U=ag_ring, S=ag_c, K=project, X=project_own, Y=project_sibling,
     )
     for letter, digit in zip(ORDER[::2], ORDER[1::2]):
         stages[letter](int(digit))
@@ -503,6 +518,8 @@
     arrived(r1by.at[0, 0, pl.ds(0, 3)], sz3r)
     total(low, pl.ds(0, 256), [rz3[k] for k in range(3)])
     total(mid, lo, [rzb3[k] for k in range(3)])
+
+    store_keys().wait()
 
     for ref, sem in (
         (r1by.at[0, pl.ds(0, 7), pl.ds(0, 2)], ag1s), (rz3, z1s), (rz2, z2s), (pieces(28), zrs),
@@ -540,7 +557,7 @@
             jax.ShapeDtypeStruct((64, 256), F32),
         ),
         in_specs=[any_spec, any_spec, any_spec],
-        out_specs=(vmem, vmem),
+        out_specs=(any_spec, vmem),
         scratch_shapes=[
             pltpu.VMEM((16, 640, 512), BF),
             pltpu.VMEM((640, 512), BF),
@@ -564,7 +581,8 @@
             pltpu.VMEM((3, 16, 256), BF),
             pltpu.VMEM((3, 16, 128), BF),
             pltpu.VMEM((640, 512), F32),
-            dma((8,)), dma, dma,
+            pltpu.VMEM((2, 320, 512), BF),
+            dma((8,)), dma, dma, dma,
             dma, dma((8,)), dma, dma((8,)), dma, dma((8,)),
             dma, dma((8,)), dma, dma((8,)),
             dma, dma, dma, dma, dma, dma((2, 5)),

time: 56.2 us -> 56 us (level)
  no operation moved by 1% of the time
where the time goes in v3:
time: 56 us; the launch traced here: 55.7 us
  Pallas kernels  55.1 us (98%)
  between operations  0.64 us (1%)
    pallas_call x1, Pallas kernels, per_device(): pl.pallas_call(functools.partial(kernel, gscale), out_shape=(jax.ShapeDty...  53 us
    pallas_call x1, Pallas kernels, per_device(): pl.pallas_call(update, out_shape=(jax.ShapeDtypeStruct((2, 320, 512), BF)...  2.12 us

profile of v3, /device:TPU:1, one launch (start us, length us, event | category | flops | bytes accessed | tf_op | source)
XLA Modules:
  0.0 55.7 jit_solution(17098704713316350336)
XLA Ops:
  0.6 53.0 %project_and_reduce.1 = (bf16[2,320,512]{2,1,0:T(8,128)(2,1)}, f32[64,256]{1,0:T(8,128)}) custom-call(bf16[2,320,8192]{2,1,0:T(8,128)(2,1)} %a_hbm.1, bf16[2,320,512]{2,1,0:T(8,128)(2,1)} %c_hbm.1, f32[64,256]{1,0:T(8,128)} %bitcast.6), custom_call_target="tpu_custom_call" | custom-call | flops 10737418240 | bytes 12582912 | tf_op jit(solution)/shard_map/project_and_reduce/pallas_call | solution.py:553
  53.6 2.1 %adam_update.1 = (bf16[2,320,512]{2,1,0:T(8,128)(2,1)}, f32[64,256]{1,0:T(8,128)}, f32[64,256]{1,0:T(8,128)}, f32[64,256]{1,0:T(8,128)}) custom-call(bf16[2,320,512]{2,1,0:T(8,128)(2,1)} %get-tuple-element.10.keys_ref, f32[64,256]{1,0:T(8,128)} %get-tuple-element.11.grad_ref, f32[64,256]{1,0:T(8,128)} %bitcast.7, f32[64,256]{1,0:T(8,128)} %bitcast.8, ...), custom_call_target="tpu_custom_call" | custom-call | tf_op jit(solution)/shard_map/adam_update/pallas_call | solution.py:601

commit v4 on v3

--- a/solution.py
+++ b/solution.py
@@ -489,14 +489,14 @@
 
     load_m.wait()
     wt[yh, z, c, x, yl] = mb[...].astype(BF)
-    arrived(cb, sem_c)
-    ct[...] = cb[...].T
     pl.semaphore_wait(barrier, len(partners))
     for d in (1, 3, 2):
         agz1(d).start()
     for d in (1, 7, 2, 6, 3, 5, 4):
         ag1(d).start()
     ag_second(0)
+    arrived(cb, sem_c)
+    ct[...] = cb[...].T
 
     stages = dict(
         T=rs_terms, P=rs_pair, R=rs_ring, B=rs_pass, C=rs_second, D=rs_third, L=rz_last,

time: 56 us -> 56.1 us (level)
  no operation moved by 1% of the time
where the time goes in v4:
time: 56.1 us; the launch traced here: 56 us
  Pallas kernels  55.4 us (99%)
  between operations  0.64 us (1%)
    pallas_call x1, Pallas kernels, per_device(): pl.pallas_call(functools.partial(kernel, gscale), out_shape=(jax.ShapeDty...  53.2 us
    pallas_call x1, Pallas kernels, per_device(): pl.pallas_call(update, out_shape=(jax.ShapeDtypeStruct((2, 320, 512), BF)...  2.12 us

profile of v4, /device:TPU:1, one launch (start us, length us, event | category | flops | bytes accessed | tf_op | source)
XLA Modules:
  0.0 56.0 jit_solution(4332885180180268022)
XLA Ops:
  0.6 53.2 %project_and_reduce.1 = (bf16[2,320,512]{2,1,0:T(8,128)(2,1)}, f32[64,256]{1,0:T(8,128)}) custom-call(bf16[2,320,8192]{2,1,0:T(8,128)(2,1)} %a_hbm.1, bf16[2,320,512]{2,1,0:T(8,128)(2,1)} %c_hbm.1, f32[64,256]{1,0:T(8,128)} %bitcast.6), custom_call_target="tpu_custom_call" | custom-call | flops 10737418240 | bytes 12582912 | tf_op jit(solution)/shard_map/project_and_reduce/pallas_call | solution.py:553
  53.9 2.1 %adam_update.1 = (bf16[2,320,512]{2,1,0:T(8,128)(2,1)}, f32[64,256]{1,0:T(8,128)}, f32[64,256]{1,0:T(8,128)}, f32[64,256]{1,0:T(8,128)}) custom-call(bf16[2,320,512]{2,1,0:T(8,128)(2,1)} %get-tuple-element.10.keys_ref, f32[64,256]{1,0:T(8,128)} %get-tuple-element.11.grad_ref, f32[64,256]{1,0:T(8,128)} %bitcast.7, f32[64,256]{1,0:T(8,128)} %bitcast.8, ...), custom_call_target="tpu_custom_call" | custom-call | tf_op jit(solution)/shard_map/adam_update/pallas_call | solution.py:601
